TPU v7x, 32 devices: a whole 2x2x4 slice. The times are simulated.
32 devices in a mesh: grp: 2 (over y), dp: 8 (over z, x), ep: 2 (over core).
Axes of the slice: x: 2, y: 2, z: 4, core: 2. Of those that a mesh axis runs over, the one named last changes fastest.
Arguments:
- cache: bfloat16 [64, 24, 36864], P(('grp', 'dp', 'ep')), parts along dimension 0, may hold values from -4.5 to 4.5
- queries: bfloat16 [64, 1, 73728], P(('grp', 'dp', 'ep')), parts along dimension 0, may hold values from -14 to 14
- kv_new: bfloat16 [64, 1, 576], P(('grp', 'dp', 'ep')), parts along dimension 0, may hold values from -4.5 to 4.5
- lengths: int32 [64], P('grp'), parts along dimension 0, may hold values from 1 to 1535, as said below
- move_slot: int32 [32], P('grp'), parts along dimension 0, may hold values from 0 to 2, as said below
- hidden: bfloat16 [64, 1, 7168], P(('grp', 'dp', 'ep')), parts along dimension 0, may hold values from -6 to 6
- expert_ids: int32 [64, 1, 8], P('grp'), parts along dimension 0, may hold values from 0 to 15, all different within a row
- router: bfloat16 [16, 7168], replicated, may hold values from -0.0625 to 0.0625
- routed_gate: bfloat16 [16384, 7168], P(('dp', 'ep')), may hold values from -0.0625 to 0.0625
- routed_up: bfloat16 [16384, 7168], P(('dp', 'ep')), may hold values from -0.0625 to 0.0625
- routed_down: bfloat16 [16384, 7168], P(('dp', 'ep')), may hold values from -0.1875 to 0.1875
- shared_gate: bfloat16 [2048, 7168], P(('dp', 'ep')), may hold values from -0.0625 to 0.0625
- shared_up: bfloat16 [2048, 7168], P(('dp', 'ep')), may hold values from -0.0625 to 0.0625
- shared_down: bfloat16 [2048, 7168], P(('dp', 'ep')), may hold values from -0.125 to 0.125
Outputs:
- attn_out: bfloat16 [64, 1, 65536], P(('grp', 'dp', 'ep')), parts along dimension 0
- moe_out: bfloat16 [64, 1, 7168], P(('grp', 'dp', 'ep')), parts along dimension 0
There are 2 independent parts, one for each index of `grp`. A program takes and returns all parts, laid end to end along the dimension named above; an argument that names none is the same for every part. Nothing has to cross between parts.
Inputs may be any that keep to these rules, and one draw needn't show every extreme that they name: `lengths`: positions of a slot's cache at or above its length hold no data. `move_slot`: 2 means that no request of the group moves; a group and its partner are both 2 or both below it.
All inputs are finite; a program needn't handle non-finite values.
Results may differ from a plain program's by a relative error of at most 0.009.
Values may be sent and summed in bfloat16 or wider, within the bound.
A program may use at most 128 MiB of HBM per device.

v0:
```python
import functools

import jax
import jax.numpy as jnp
from jax import lax
from jax.experimental import pallas as pl
from jax.experimental.pallas import tpu as pltpu
from jax.sharding import PartitionSpec as P

DL = 512
FF = 1024
SCORE_SCALE = 192.0 ** (-0.5)
ROUTE_SCALE = 2.5
NEGATIVE = -1e30
CH = 8
WIDTHS = (384, 256, 256)
MESH = pl.DeviceIdType.MESH
F32 = jnp.float32
BF16 = jnp.bfloat16


def contract_last(a, b):
    return lax.dot_general(a, b, (((1,), (1,)), ((), ())), preferred_element_type=F32)


def kernel(
    n_dp, rchunk,
    scal, qk_ref, hid_ref, ids_ref, pos_ref,
    cache_h, router_h, rg_h, ru_h, rd_h, sg_h, su_h, sd_h,
    attn_ref, moe_ref,
    cache_s, router_s, g_s, u_s, d_s,
    xg, xf, x_s, act_s, kk, qsend, qrecv, osend, orecv,
    ybuf, yown, r1, zs, fs, zb0, zb1, zb2, q20, q21, q22,
    w_sem, sx, sf, rx, sq, rq, so, ro, s1, rr1, s2, r2sem,
):
    j0 = lax.axis_index("dp")
    e0 = lax.axis_index("ep")
    sib = 1 - e0
    partner = lax.rem(j0 + n_dp // 2, n_dp)
    rows = rg_h.shape[0]
    srows = sg_h.shape[0]
    d_model = rg_h.shape[1]
    ntok = x_s.shape[0]
    half = ntok // 2
    zbs, r2s = (zb0, zb1, zb2), (q20, q21, q22)

    copies = []

    def fetch(src, dst):
        c = pltpu.make_async_copy(src, dst, w_sem.at[len(copies)])
        c.start()
        copies.append(c)
        return c

    c_cache = fetch(cache_h, cache_s)
    c_router = fetch(router_h, router_s)
    gu = []
    for r in range(0, rows, rchunk):
        gu.append((
            r, rchunk, True,
            fetch(rg_h.at[pl.ds(r, rchunk), :], g_s.at[pl.ds(r, rchunk), :]),
            fetch(ru_h.at[pl.ds(r, rchunk), :], u_s.at[pl.ds(r, rchunk), :]),
        ))
    gu.append((
        rows, srows, False,
        fetch(sg_h, g_s.at[pl.ds(rows, srows), :]),
        fetch(su_h, u_s.at[pl.ds(rows, srows), :]),
    ))
    downs = []
    base = 0
    for w in WIDTHS:
        cols = pl.ds(base, CH * w)
        downs.append((
            base, w,
            fetch(rd_h.at[:, cols], d_s.at[pl.ds(0, rows), cols]),
            fetch(sd_h.at[:, cols], d_s.at[pl.ds(rows, srows), cols]),
        ))
        base += CH * w

    barrier = pltpu.get_barrier_semaphore()

    def greet(k, _):
        pl.semaphore_signal(barrier, inc=1, device_id={"dp": lax.rem(j0 + k, n_dp)}, device_id_type=MESH)
        return 0

    lax.fori_loop(1, n_dp, greet, 0)
    pl.semaphore_signal(barrier, inc=1, device_id={"ep": sib}, device_id_type=MESH)
    pl.semaphore_wait(barrier, n_dp)

    def x_copy(k):
        return pltpu.make_async_remote_copy(
            src_ref=hid_ref, dst_ref=xg.at[e0, j0], send_sem=sx.at[k], recv_sem=rx.at[e0, j0],
            device_id={"dp": lax.rem(j0 + k, n_dp)}, device_id_type=MESH)

    x_sib = pltpu.make_async_remote_copy(
        src_ref=hid_ref, dst_ref=xg.at[e0, j0], send_sem=sx.at[0], recv_sem=rx.at[e0, j0],
        device_id={"ep": sib}, device_id_type=MESH)

    def x_send(k, _):
        x_copy(k).start()
        return 0

    lax.fori_loop(1, n_dp, x_send, 0)
    x_sib.start()
    xg[e0, j0] = hid_ref[...]

    own_move = scal[0]
    moving = own_move < 2
    slot_b = jnp.where(own_move == 0, 0, 1)
    slot_a = 1 - slot_b
    nq = qsend.shape[0] - 16
    pairs = kk.shape[0] // cache_s.shape[1]
    pages = cache_s.shape[1]
    wide = kk.shape[1]
    win = (wide // 2 + 127) // 128 * 128
    off = wide - win
    shift = wide // 2 - off
    dk = wide // 2

    def attend(qk, slot, length):
        def retile(t, _):
            parts = [
                cache_s[slot, :, pl.ds(pl.multiple_of((2 * t + i) * wide, 128), wide)].astype(F32)
                for i in range(2)
            ]
            kk[pl.ds(pl.multiple_of(2 * pages * t, 16), 2 * pages), :] = (
                jnp.concatenate(parts, axis=0).astype(BF16))
            return 0

        lax.fori_loop(0, pairs // 2, retile, 0)
        qf = qk.astype(F32)
        lane = lax.broadcasted_iota(jnp.int32, (nq, win), 1)
        q_even = jnp.where(lane < dk, qf[:nq, :win], 0.0)
        q_odd = jnp.where(lane >= shift, qf[:nq, off:], 0.0)
        qe = jnp.concatenate([q_even, pltpu.roll(q_odd, win - shift, 1)], axis=0)
        qo = jnp.concatenate([pltpu.roll(q_even, shift, 1), q_odd], axis=0)
        kv = qf[nq:nq + 1, :win]
        s_n = jnp.sum(qe * kv, axis=1, keepdims=True) * SCORE_SCALE
        pos = pos_ref[0:1, :]
        s_e = jnp.where(pos < length, contract_last(qe.astype(BF16), kk[:, :win]) * SCORE_SCALE, NEGATIVE)
        s_o = jnp.where(pos + 1 < length, contract_last(qo.astype(BF16), kk[:, off:]) * SCORE_SCALE, NEGATIVE)
        top = jnp.maximum(jnp.max(s_e, axis=1, keepdims=True), jnp.max(s_o, axis=1, keepdims=True))
        top = jnp.maximum(top, s_n)
        p_e, p_o, p_n = jnp.exp(s_e - top), jnp.exp(s_o - top), jnp.exp(s_n - top)
        total = jnp.sum(p_e, axis=1, keepdims=True) + jnp.sum(p_o, axis=1, keepdims=True) + p_n
        o_e = jnp.dot(p_e.astype(BF16), kk[:, :DL], preferred_element_type=F32)
        o_o = jnp.dot(p_o.astype(BF16), kk[:, off:], preferred_element_type=F32)
        out = o_e + pltpu.roll(o_o, win - shift, 1)[:, :DL] + p_n * kv[:, :DL]
        out = out / total
        return jnp.concatenate([out[:nq], out[nq:]], axis=1).astype(BF16)

    qsend[...] = qk_ref[slot_b]
    c_cache.wait()
    out_a = attend(qk_ref[slot_a], slot_a, scal[1 + slot_a])
    attn_ref[0] = out_a

    def arrived(e, j):
        return pltpu.make_async_remote_copy(
            src_ref=hid_ref, dst_ref=xg.at[e, j], send_sem=sx.at[0], recv_sem=rx.at[e, j],
            device_id={"ep": sib}, device_id_type=MESH)

    def fwd_copy(k):
        j = lax.rem(j0 + n_dp - k, n_dp)
        return pltpu.make_async_remote_copy(
            src_ref=xg.at[e0, j], dst_ref=xg.at[e0, j], send_sem=sf.at[k], recv_sem=rx.at[e0, j],
            device_id={"ep": sib}, device_id_type=MESH)

    def pass_on(k, _):
        arrived(e0, lax.rem(j0 + n_dp - k, n_dp)).wait_recv()
        fwd_copy(k).start()
        return 0

    lax.fori_loop(1, n_dp, pass_on, 0)

    q_copy = pltpu.make_async_remote_copy(
        src_ref=qsend, dst_ref=qrecv, send_sem=sq, recv_sem=rq,
        device_id={"dp": partner}, device_id_type=MESH)
    q_copy.start()

    def settle(k, _):
        arrived(sib, lax.rem(j0 + n_dp - k, n_dp)).wait_recv()
        return 0

    lax.fori_loop(0, n_dp, settle, 0)

    tiles = xf.shape[0]
    gathered = xg[...].reshape(xf.shape[1], tiles * 128).astype(F32)
    for i in range(tiles):
        xf[i] = gathered[:, i * 128:(i + 1) * 128]
    for c in range(CH):
        for i in range(tiles):
            at = (c * tiles + i) * 128
            x_s[:, at:at + 128] = xf[i, pl.ds(c, ntok, stride=CH), :].astype(BF16)

    c_router.wait()
    n_exp = router_s.shape[0]
    sig = 1.0 / (1.0 + jnp.exp(-contract_last(x_s[...], router_s[...])))
    table = lax.broadcasted_iota(jnp.int32, (ntok, n_exp), 1)
    ids = ids_ref[...]
    chosen = jnp.zeros((ntok, n_exp), F32)
    for k in range(ids.shape[1]):
        chosen += jnp.where(ids[:, k:k + 1] == table, 1.0, 0.0)
    picked = sig * chosen
    expert = (j0 * 2 + e0) * rows // FF
    mine = jnp.sum(jnp.where(table == expert, picked, 0.0), axis=1, keepdims=True)
    row_weight = ROUTE_SCALE * mine / jnp.sum(picked, axis=1, keepdims=True)

    for r, n, routed, cg, cu in gu:
        cg.wait()
        g = contract_last(x_s[...], g_s[pl.ds(r, n), :])
        cu.wait()
        u = contract_last(x_s[...], u_s[pl.ds(r, n), :])
        act = g / (1.0 + jnp.exp(-g)) * u
        if routed:
            act = row_weight * act
        act_s[:, r:r + n] = act.astype(BF16)

    q_copy.wait_recv()
    q_b = jnp.where(moving, qrecv[...].astype(F32), qsend[...].astype(F32)).astype(BF16)
    out_b = attend(q_b, slot_b, scal[1 + slot_b])
    osend[...] = out_b
    o_copy = pltpu.make_async_remote_copy(
        src_ref=osend, dst_ref=orecv, send_sem=so, recv_sem=ro,
        device_id={"dp": partner}, device_id_type=MESH)
    o_copy.start()

    def first_copy(p):
        b, w = downs[p][0], downs[p][1]
        cols = pl.ds(b, CH * w)
        return pltpu.make_async_remote_copy(
            src_ref=ybuf.at[pl.ds(pl.multiple_of(sib * half, 16), half), cols],
            dst_ref=r1.at[:, cols], send_sem=s1.at[p], recv_sem=rr1.at[p],
            device_id={"ep": sib}, device_id_type=MESH)

    def second_copy(p, k):
        j = lax.rem(j0 + k, n_dp)
        return pltpu.make_async_remote_copy(
            src_ref=zbs[p].at[j], dst_ref=r2s[p].at[j0], send_sem=s2.at[p, k], recv_sem=r2sem.at[p, j0],
            device_id={"dp": j}, device_id_type=MESH)

    def second_arrived(p, j):
        return pltpu.make_async_remote_copy(
            src_ref=zbs[p].at[j], dst_ref=r2s[p].at[j], send_sem=s2.at[p, 0], recv_sem=r2sem.at[p, j],
            device_id={"dp": j}, device_id_type=MESH)

    def combine(p):
        b, w = downs[p][0], downs[p][1]
        first_copy(p).wait_recv()
        z = yown[:, b:b + CH * w] + r1[:, b:b + CH * w].astype(F32)
        for c in range(CH):
            for i in range(w // 128):
                at = c * w + i * 128
                zs[i, pl.ds(c, half, stride=CH), :] = z[:, at:at + 128]
        for i in range(w // 128):
            zbs[p][:, :, i * 128:(i + 1) * 128] = zs[i].astype(BF16).reshape(n_dp, -1, 128)

        def send(k, _):
            second_copy(p, k).start()
            return 0

        lax.fori_loop(1, n_dp, send, 0)

    def finish(p):
        b, w = downs[p][0], downs[p][1]

        def add(k, total):
            j = lax.rem(j0 + k, n_dp)
            second_arrived(p, j).wait_recv()
            return total + r2s[p][j].astype(F32)

        total = lax.fori_loop(1, n_dp, add, zbs[p][j0].astype(F32))
        for i in range(w // 128):
            fs[i] = total[:, i * 128:(i + 1) * 128]
        for c in range(CH):
            for i in range(w // 128):
                at = b + c * w + i * 128
                moe_ref[:, at:at + 128] = fs[i, pl.ds(c, fs.shape[1] // CH, stride=CH), :]

    act_all = act_s[...]
    for p, (b, w, c1, c2) in enumerate(downs):
        c1.wait()
        c2.wait()
        y = jnp.dot(act_all, d_s[:, b:b + CH * w], preferred_element_type=F32)
        ybuf[:, b:b + CH * w] = y.astype(BF16)
        yown[:, b:b + CH * w] = jnp.where(e0 == 0, y[:half], y[half:])
        first_copy(p).start()
        if p > 0:
            combine(p - 1)
    combine(len(downs) - 1)
    for p in range(len(downs)):
        finish(p)

    o_copy.wait_recv()
    res_a = attn_ref[0].astype(F32)
    res_b = jnp.where(moving, orecv[...].astype(F32), osend[...].astype(F32))
    attn_ref[0] = jnp.where(slot_a == 0, res_a, res_b).astype(BF16)
    attn_ref[1] = jnp.where(slot_a == 0, res_b, res_a).astype(BF16)

    x_sib.wait_send()
    q_copy.wait_send()
    o_copy.wait_send()

    def drain(k, _):
        x_copy(k).wait_send()
        fwd_copy(k).wait_send()
        for p in range(len(downs)):
            second_copy(p, k).wait_send()
        return 0

    lax.fori_loop(1, n_dp, drain, 0)
    for p in range(len(downs)):
        first_copy(p).wait_send()


def local(cache, queries, kv_new, lengths, move_slot, hidden, expert_ids, router,
          routed_gate, routed_up, routed_down, shared_gate, shared_up, shared_down):
    n_dp = lax.axis_size("dp")
    n_ep = lax.axis_size("ep")
    slots, pages, page_len = cache.shape
    dk = kv_new.shape[-1]
    d_model = hidden.shape[-1]
    own_tok = hidden.shape[0] * hidden.shape[1]
    ntok = own_tok * n_dp * n_ep
    half = ntok // 2
    rows, srows = routed_gate.shape[0], shared_gate.shape[0]
    all_rows = rows + srows
    wide = 2 * dk
    nq = queries.shape[-1] // wide
    pairs = page_len // wide
    device = lax.axis_index(("dp", "ep"))
    own_lengths = lax.dynamic_slice_in_dim(lengths, device * slots, slots, 0)
    own_move = lax.dynamic_slice_in_dim(move_slot, device, 1, 0)
    scal = jnp.concatenate([own_move, own_lengths])
    kv = jnp.pad(kv_new.reshape(slots, 1, dk), ((0, 0), (0, 15), (0, wide - dk)))
    qk = jnp.concatenate([queries.reshape(slots, nq, wide), kv], axis=1)
    hid = hidden.reshape(own_tok * CH, d_model // CH)
    ids = expert_ids.reshape(n_dp, n_ep, own_tok, -1).transpose(1, 0, 2, 3).reshape(ntok, -1)
    index = jnp.arange(pairs * pages, dtype=jnp.int32)
    pos = jnp.broadcast_to((index % pages * (2 * pairs) + index // pages * 2)[None], (8, pairs * pages))
    wmax = max(WIDTHS)
    np_ = len(WIDTHS)
    rchunk = min(rows, 256)
    ncopy = 2 + 2 * (rows // rchunk + 1) + 2 * np_
    vm = pl.BlockSpec(memory_space=pltpu.VMEM)
    hb = pl.BlockSpec(memory_space=pl.ANY)
    dma = pltpu.SemaphoreType.DMA
    attn, moe = pl.pallas_call(
        functools.partial(kernel, n_dp, rchunk),
        out_shape=(
            jax.ShapeDtypeStruct((slots, nq, 2 * DL), BF16),
            jax.ShapeDtypeStruct((own_tok, d_model), F32),
        ),
        in_specs=[pl.BlockSpec(memory_space=pltpu.SMEM), vm, vm, vm, vm] + [hb] * 8,
        out_specs=(vm, vm),
        scratch_shapes=[
            pltpu.VMEM(cache.shape, BF16),
            pltpu.VMEM(router.shape, BF16),
            pltpu.VMEM((all_rows, d_model), BF16),
            pltpu.VMEM((all_rows, d_model), BF16),
            pltpu.VMEM((all_rows, d_model), BF16),
            pltpu.VMEM((n_ep, n_dp, own_tok * CH, d_model // CH), BF16),
            pltpu.VMEM((d_model // CH // 128, ntok * CH, 128), F32),
            pltpu.VMEM((ntok, d_model), BF16),
            pltpu.VMEM((ntok, all_rows), BF16),
            pltpu.VMEM((pairs * pages, wide), BF16),
            pltpu.VMEM((nq + 16, wide), BF16),
            pltpu.VMEM((nq + 16, wide), BF16),
            pltpu.VMEM((nq, 2 * DL), BF16),
            pltpu.VMEM((nq, 2 * DL), BF16),
            pltpu.VMEM((ntok, d_model), BF16),
            pltpu.VMEM((half, d_model), F32),
            pltpu.VMEM((half, d_model), BF16),
            pltpu.VMEM((wmax // 128, half * CH, 128), F32),
            pltpu.VMEM((wmax // 128, own_tok * CH, 128), F32),
        ]
        + [pltpu.VMEM((n_dp, own_tok * CH, w), BF16) for w in WIDTHS] * 2
        + [
            dma((ncopy,)), dma((n_dp,)), dma((n_dp,)), dma((n_ep, n_dp)),
            dma, dma, dma, dma,
            dma((np_,)), dma((np_,)), dma((np_, n_dp)), dma((np_, n_dp)),
        ],
        compiler_params=pltpu.CompilerParams(
            collective_id=0, has_side_effects=True, vmem_limit_bytes=63 * 1024 * 1024),
    )(scal, qk, hid, ids, pos, cache, router, routed_gate, routed_up, routed_down,
      shared_gate, shared_up, shared_down)
    return (attn.reshape(slots, 1, nq * 2 * DL), moe.astype(BF16).reshape(hidden.shape))


def solution(mesh):
    row = P(("grp", "dp", "ep"), None, None)
    weight = P(("dp", "ep"), None)
    in_specs = (row, row, row, P("grp"), P("grp"), row, P("grp", None, None), P()) + (weight,) * 6
    return jax.shard_map(local, mesh=mesh, in_specs=in_specs, out_specs=(row, row), check_vma=False)
```

profile of v0, /device:TPU:0, one launch (start us, length us, event | category | flops | bytes accessed | tf_op | source)
XLA Modules:
  0.0 63.5 jit_solution(18024854670188486912)
XLA Ops:
  0.6 1.2 %dynamic_slice.6 = s32[1]{0:T(128)} dynamic-slice(s32[16]{0:T(128)} %param.18, s32[]{:T(128)S(6)} %select_n.26), dynamic_slice_sizes={1} | dynamic-slice | bytes 12 | tf_op jit(solution)/shard_map/dynamic_slice | solution.py:332
  1.9 0.7 %dynamic_slice.7 = s32[2]{0:T(128)S(1)} dynamic-slice(s32[32]{0:T(128)} %param.17, s32[]{:T(128)S(6)} %select_n.27), dynamic_slice_sizes={2} | dynamic-slice | bytes 20 | tf_op jit(solution)/shard_map/dynamic_slice | solution.py:331
  2.6 1.2 %pad_add_fusion.scal = s32[3]{0:T(128)} fusion(s32[2]{0:T(128)S(1)} %dynamic_slice.7, s32[1]{0:T(128)} %dynamic_slice.6), kind=kLoop, calls=%fused_computation.19 | loop fusion | flops 3 | bytes 24 | tf_op jit(solution)/shard_map/concatenate | solution.py:333
  3.9 0.7 %copy.18 = bf16[2,1,576]{2,1,0:T(2,128)(2,1)S(1)} copy(bf16[2,1,576]{2,0,1:T(2,128)(2,1)} %param.16) | data formatting | bytes 4608 | tf_op args[2]
  4.5 0.8 %copy.19 = s32[32,1,8]{2,0,1:T(8,128)S(1)} copy(s32[32,1,8]{0,2,1:T(8,128)} %param.20) | data formatting | bytes 2048 | tf_op args[6]
  5.3 0.6 copy.20
  5.9 0.6 broadcast_in_dim.2.pos_ref
  6.5 1.4 %reshape.43.hid_ref = bf16[16,896]{1,0:T(8,128)(2,1)} reshape(bf16[2,1,7168]{2,0,1:T(2,128)(2,1)} %param.19) | data formatting | bytes 57344 | tf_op jit(solution)/shard_map/reshape | solution.py:336
  7.9 1.0 %copy.23 = bf16[1,2,64,1152]{3,2,1,0:T(8,128)(2,1)S(1)} copy(bf16[1,2,64,1152]{3,1,2,0:T(2,128)(2,1)} %bitcast.15) | data formatting | bytes 589824
  8.9 0.8 %fusion.1.qk_ref = bf16[2,80,1152]{2,1,0:T(8,128)(2,1)} fusion(bf16[2,1,576]{2,1,0:T(2,128)(2,1)S(1)} %copy.18, bf16[2,64,1152]{2,1,0:T(8,128)(2,1)S(1)} %bitcast.14), kind=kLoop, calls=%fused_computation.2 | loop fusion | flops 1105920 | bytes 665856 | tf_op jit(solution)/shard_map/concatenate | solution.py:335
  9.7 50.5 %shard_map.149 = (bf16[2,64,1024]{2,1,0:T(8,128)(2,1)}, f32[2,7168]{1,0:T(2,128)}) custom-call(s32[3]{0:T(128)} %pad_add_fusion.scal, bf16[2,80,1152]{2,1,0:T(8,128)(2,1)} %fusion.1.qk_ref, bf16[16,896]{1,0:T(8,128)(2,1)} %reshape.43.hid_ref, s32[32,8]{1,0:T(8,128)} %bitcast.16, s32[8,768]{1,0:T(8,128)} %broadcast_in_dim.2.pos_ref, ...), custom_call_target="tpu_custom_call" | custom-call | tf_op jit(solution)/shard_map/pallas_call | solution.py:347
  60.2 1.9 %reshape.46 = bf16[2,1,65536]{2,0,1:T(2,128)(2,1)} reshape(bf16[2,64,1024]{2,1,0:T(8,128)(2,1)} %get-tuple-element.4) | data formatting | bytes 524288 | tf_op jit(solution)/shard_map/reshape | solution.py:386
  62.0 1.4 %convert_bitcast_fusion = bf16[2,1,7168]{2,0,1:T(2,128)(2,1)} fusion(f32[2,7168]{1,0:T(2,128)} %get-tuple-element.5), kind=kLoop, calls=%fused_computation.4 | loop fusion | flops 14336 | bytes 86016 | tf_op jit(solution)/shard_map/reshape | solution.py:386
  (1 shorter events, 0.0 us)
where the time goes:
time: 63.9 us; the launch traced here: 63.5 us
  Pallas kernels  50.5 us (79%)
  local copies, waits for them, and re-layouts  8.86 us (14%)
  other arithmetic  3.46 us (5%)
  between operations  0.65 us (1%)
    pallas_call x1, Pallas kernels, local(): pl.pallas_call(functools.partial(kernel, n_dp, rchunk), out_shape=(jax.Sh...  50.5 us
    unnamed x3, local copies, waits for them, and re-layouts  2.44 us
    reshape x1, local copies, waits for them, and re-layouts, local(): attn.reshape(slots, 1, nq * 2 * DL)  1.85 us
    reshape x1, other arithmetic, local(): moe.astype(BF16).reshape(hidden.shape)  1.45 us
    reshape x1, local copies, waits for them, and re-layouts, local(): hid = hidden.reshape(own_tok * CH, d_model // CH)  1.38 us

commit v1 on v0

--- a/solution.py
+++ b/solution.py
@@ -25,13 +25,13 @@
 
 def kernel(
     n_dp, rchunk,
-    scal, qk_ref, hid_ref, ids_ref, pos_ref,
+    len_ref, move_ref, q_ref, kv_ref, hid_ref, ids_ref,
     cache_h, router_h, rg_h, ru_h, rd_h, sg_h, su_h, sd_h,
     attn_ref, moe_ref,
     cache_s, router_s, g_s, u_s, d_s,
-    xg, xf, x_s, act_s, kk, qsend, qrecv, osend, orecv,
+    hf, hsend, xg, xf, x_s, act_s, kk, qsend, qrecv, kvsend, kvrecv, osend, orecv,
     ybuf, yown, r1, zs, fs, zb0, zb1, zb2, q20, q21, q22,
-    w_sem, sx, sf, rx, sq, rq, so, ro, s1, rr1, s2, r2sem,
+    w_sem, sx, sf, sg, rx, sq, rq, skv, rkv, so, ro, s1, rr1, s2, r2sem,
 ):
     j0 = lax.axis_index("dp")
     e0 = lax.axis_index("ep")
@@ -77,6 +77,16 @@
         ))
         base += CH * w
 
+    tiles = hf.shape[0]
+    own = hid_ref[...].astype(F32)
+    own_tok = own.shape[0]
+    for c in range(CH):
+        for i in range(tiles):
+            at = (c * tiles + i) * 128
+            hf[i, pl.ds(c, own_tok, stride=CH), :] = own[:, at:at + 128]
+    for i in range(tiles):
+        hsend[:, i * 128:(i + 1) * 128] = hf[i].astype(BF16)
+
     barrier = pltpu.get_barrier_semaphore()
 
     def greet(k, _):
@@ -87,28 +97,50 @@
     pl.semaphore_signal(barrier, inc=1, device_id={"ep": sib}, device_id_type=MESH)
     pl.semaphore_wait(barrier, n_dp)
 
-    def x_copy(k):
+    n_out = n_dp // 2
+    out0 = j0 // 2
+    in0 = lax.rem(j0, 2)
+    across = out0 * 2 + 1 - in0
+
+    def peer(k):
+        return lax.rem(out0 + k, n_out) * 2 + in0
+
+    def x_copy(src, j, sem, target):
         return pltpu.make_async_remote_copy(
-            src_ref=hid_ref, dst_ref=xg.at[e0, j0], send_sem=sx.at[k], recv_sem=rx.at[e0, j0],
-            device_id={"dp": lax.rem(j0 + k, n_dp)}, device_id_type=MESH)
-
-    x_sib = pltpu.make_async_remote_copy(
-        src_ref=hid_ref, dst_ref=xg.at[e0, j0], send_sem=sx.at[0], recv_sem=rx.at[e0, j0],
-        device_id={"ep": sib}, device_id_type=MESH)
-
-    def x_send(k, _):
-        x_copy(k).start()
-        return 0
-
-    lax.fori_loop(1, n_dp, x_send, 0)
-    x_sib.start()
-    xg[e0, j0] = hid_ref[...]
-
-    own_move = scal[0]
+            src_ref=src, dst_ref=xg.at[e0, j], send_sem=sem, recv_sem=rx.at[e0, j],
+            device_id=target, device_id_type=MESH)
+
+    def x_out(k):
+        return x_copy(hsend, j0, sx.at[k], {"dp": peer(k)})
+
+    def x_over(k):
+        src = hsend if k is None else xg.at[e0, peer(k)]
+        j = j0 if k is None else peer(k)
+        return x_copy(src, j, sf.at[0 if k is None else k], {"dp": across})
+
+    def x_sib(j, src):
+        return x_copy(src, j, sg.at[j], {"ep": sib})
+
+    def arrived(e, j):
+        return pltpu.make_async_remote_copy(
+            src_ref=hsend, dst_ref=xg.at[e, j], send_sem=sx.at[0], recv_sem=rx.at[e, j],
+            device_id={"ep": sib}, device_id_type=MESH)
+
+    def send_out(k, _):
+        x_out(k).start()
+        return 0
+
+    lax.fori_loop(1, n_out, send_out, 0)
+    x_over(None).start()
+    x_sib(j0, hsend).start()
+    xg[e0, j0] = hsend[...]
+
+    device = j0 * 2 + e0
+    own_move = move_ref[device]
     moving = own_move < 2
     slot_b = jnp.where(own_move == 0, 0, 1)
     slot_a = 1 - slot_b
-    nq = qsend.shape[0] - 16
+    nq = qsend.shape[0]
     pairs = kk.shape[0] // cache_s.shape[1]
     pages = cache_s.shape[1]
     wide = kk.shape[1]
@@ -117,7 +149,9 @@
     shift = wide // 2 - off
     dk = wide // 2
 
-    def attend(qk, slot, length):
+    def attend(q, kv, slot):
+        length = len_ref[device * 2 + slot]
+
         def retile(t, _):
             parts = [
                 cache_s[slot, :, pl.ds(pl.multiple_of((2 * t + i) * wide, 128), wide)].astype(F32)
@@ -128,15 +162,16 @@
             return 0
 
         lax.fori_loop(0, pairs // 2, retile, 0)
-        qf = qk.astype(F32)
+        qf = q.astype(F32)
         lane = lax.broadcasted_iota(jnp.int32, (nq, win), 1)
         q_even = jnp.where(lane < dk, qf[:nq, :win], 0.0)
         q_odd = jnp.where(lane >= shift, qf[:nq, off:], 0.0)
         qe = jnp.concatenate([q_even, pltpu.roll(q_odd, win - shift, 1)], axis=0)
         qo = jnp.concatenate([pltpu.roll(q_even, shift, 1), q_odd], axis=0)
-        kv = qf[nq:nq + 1, :win]
         s_n = jnp.sum(qe * kv, axis=1, keepdims=True) * SCORE_SCALE
-        pos = pos_ref[0:1, :]
+        index = lax.broadcasted_iota(jnp.int32, (1, kk.shape[0]), 1)
+        pair = ((index.astype(F32) + 0.5) * (1.0 / pages)).astype(jnp.int32)
+        pos = (index - pair * pages) * (2 * pairs) + pair * 2
         s_e = jnp.where(pos < length, contract_last(qe.astype(BF16), kk[:, :win]) * SCORE_SCALE, NEGATIVE)
         s_o = jnp.where(pos + 1 < length, contract_last(qo.astype(BF16), kk[:, off:]) * SCORE_SCALE, NEGATIVE)
         top = jnp.maximum(jnp.max(s_e, axis=1, keepdims=True), jnp.max(s_o, axis=1, keepdims=True))
@@ -149,33 +184,35 @@
         out = out / total
         return jnp.concatenate([out[:nq], out[nq:]], axis=1).astype(BF16)
 
-    qsend[...] = qk_ref[slot_b]
-    c_cache.wait()
-    out_a = attend(qk_ref[slot_a], slot_a, scal[1 + slot_a])
-    attn_ref[0] = out_a
-
-    def arrived(e, j):
-        return pltpu.make_async_remote_copy(
-            src_ref=hid_ref, dst_ref=xg.at[e, j], send_sem=sx.at[0], recv_sem=rx.at[e, j],
-            device_id={"ep": sib}, device_id_type=MESH)
-
-    def fwd_copy(k):
-        j = lax.rem(j0 + n_dp - k, n_dp)
-        return pltpu.make_async_remote_copy(
-            src_ref=xg.at[e0, j], dst_ref=xg.at[e0, j], send_sem=sf.at[k], recv_sem=rx.at[e0, j],
-            device_id={"ep": sib}, device_id_type=MESH)
-
-    def pass_on(k, _):
-        arrived(e0, lax.rem(j0 + n_dp - k, n_dp)).wait_recv()
-        fwd_copy(k).start()
-        return 0
-
-    lax.fori_loop(1, n_dp, pass_on, 0)
-
+    qsend[...] = q_ref[slot_b]
+    kvs = jnp.concatenate([kv_ref[...].astype(F32), jnp.zeros((kv_ref.shape[0], win - dk), F32)], axis=1)
+    kv_b = jnp.where(slot_b == 0, kvs[0:1], kvs[1:2])
+    kv_a = jnp.where(slot_b == 0, kvs[1:2], kvs[0:1])
+    kvsend[...] = jnp.broadcast_to(kv_b, kvsend.shape).astype(BF16)
     q_copy = pltpu.make_async_remote_copy(
         src_ref=qsend, dst_ref=qrecv, send_sem=sq, recv_sem=rq,
         device_id={"dp": partner}, device_id_type=MESH)
+    kv_copy = pltpu.make_async_remote_copy(
+        src_ref=kvsend, dst_ref=kvrecv, send_sem=skv, recv_sem=rkv,
+        device_id={"dp": partner}, device_id_type=MESH)
+
+    def pass_out(k, _):
+        arrived(e0, peer(n_out - k)).wait_recv()
+        x_over(n_out - k).start()
+        x_sib(peer(n_out - k), xg.at[e0, peer(n_out - k)]).start()
+        return 0
+
+    lax.fori_loop(1, n_out, pass_out, 0)
+    kv_copy.start()
     q_copy.start()
+
+    def pass_in(k, _):
+        j = lax.rem(out0 + n_out - k, n_out) * 2 + 1 - in0
+        arrived(e0, j).wait_recv()
+        x_sib(j, xg.at[e0, j]).start()
+        return 0
+
+    lax.fori_loop(0, n_out, pass_in, 0)
 
     def settle(k, _):
         arrived(sib, lax.rem(j0 + n_dp - k, n_dp)).wait_recv()
@@ -183,7 +220,6 @@
 
     lax.fori_loop(0, n_dp, settle, 0)
 
-    tiles = xf.shape[0]
     gathered = xg[...].reshape(xf.shape[1], tiles * 128).astype(F32)
     for i in range(tiles):
         xf[i] = gathered[:, i * 128:(i + 1) * 128]
@@ -197,15 +233,22 @@
     sig = 1.0 / (1.0 + jnp.exp(-contract_last(x_s[...], router_s[...])))
     table = lax.broadcasted_iota(jnp.int32, (ntok, n_exp), 1)
     ids = ids_ref[...]
-    chosen = jnp.zeros((ntok, n_exp), F32)
-    for k in range(ids.shape[1]):
-        chosen += jnp.where(ids[:, k:k + 1] == table, 1.0, 0.0)
+    table_t = lax.broadcasted_iota(jnp.int32, (n_exp, ntok), 0)
+    chosen_t = jnp.zeros((n_exp, ntok), F32)
+    for k in range(ids.shape[0]):
+        chosen_t += jnp.where(ids[k:k + 1, :] == table_t, 1.0, 0.0)
+    row = lax.broadcasted_iota(jnp.int32, (ntok, ntok), 0)
+    core = jnp.where(row >= half, 1, 0)
+    rest = row - core * half
+    token = rest + (rest & ~(own_tok - 1)) + core * own_tok
+    perm = jnp.where(token == lax.broadcasted_iota(jnp.int32, (ntok, ntok), 1), 1.0, 0.0)
+    chosen = contract_last(perm.astype(BF16), chosen_t.astype(BF16))
     picked = sig * chosen
     expert = (j0 * 2 + e0) * rows // FF
     mine = jnp.sum(jnp.where(table == expert, picked, 0.0), axis=1, keepdims=True)
     row_weight = ROUTE_SCALE * mine / jnp.sum(picked, axis=1, keepdims=True)
 
-    for r, n, routed, cg, cu in gu:
+    def hidden_units(r, n, routed, cg, cu):
         cg.wait()
         g = contract_last(x_s[...], g_s[pl.ds(r, n), :])
         cu.wait()
@@ -215,14 +258,23 @@
             act = row_weight * act
         act_s[:, r:r + n] = act.astype(BF16)
 
+    early = min(2, len(gu))
+    for args in gu[:early]:
+        hidden_units(*args)
+
+    c_cache.wait()
+    kv_copy.wait_recv()
     q_copy.wait_recv()
-    q_b = jnp.where(moving, qrecv[...].astype(F32), qsend[...].astype(F32)).astype(BF16)
-    out_b = attend(q_b, slot_b, scal[1 + slot_b])
-    osend[...] = out_b
+    q_b = jnp.where(moving, qrecv[...].astype(F32), qsend[...].astype(F32))
+    kv_b = jnp.where(moving, kvrecv[0:1, :].astype(F32), kv_b)
+    osend[...] = attend(q_b, kv_b, slot_b)
     o_copy = pltpu.make_async_remote_copy(
         src_ref=osend, dst_ref=orecv, send_sem=so, recv_sem=ro,
         device_id={"dp": partner}, device_id_type=MESH)
     o_copy.start()
+
+    for args in gu[early:]:
+        hidden_units(*args)
 
     def first_copy(p):
         b, w = downs[p][0], downs[p][1]
@@ -274,7 +326,7 @@
         for c in range(CH):
             for i in range(w // 128):
                 at = b + c * w + i * 128
-                moe_ref[:, at:at + 128] = fs[i, pl.ds(c, fs.shape[1] // CH, stride=CH), :]
+                moe_ref[:, at:at + 128] = fs[i, pl.ds(c, own_tok, stride=CH), :].astype(BF16)
 
     act_all = act_s[...]
     for p, (b, w, c1, c2) in enumerate(downs):
@@ -287,22 +339,35 @@
         if p > 0:
             combine(p - 1)
     combine(len(downs) - 1)
+    out_a = attend(q_ref[slot_a], kv_a, slot_a)
     for p in range(len(downs)):
         finish(p)
 
     o_copy.wait_recv()
-    res_a = attn_ref[0].astype(F32)
+    res_a = out_a.astype(F32)
     res_b = jnp.where(moving, orecv[...].astype(F32), osend[...].astype(F32))
     attn_ref[0] = jnp.where(slot_a == 0, res_a, res_b).astype(BF16)
     attn_ref[1] = jnp.where(slot_a == 0, res_b, res_a).astype(BF16)
 
-    x_sib.wait_send()
     q_copy.wait_send()
+    kv_copy.wait_send()
     o_copy.wait_send()
+    x_over(None).wait_send()
+
+    def drain_out(k, _):
+        x_out(k).wait_send()
+        x_over(k).wait_send()
+        return 0
+
+    lax.fori_loop(1, n_out, drain_out, 0)
+
+    def drain_sib(j, _):
+        x_sib(j, hsend).wait_send()
+        return 0
+
+    lax.fori_loop(0, n_dp, drain_sib, 0)
 
     def drain(k, _):
-        x_copy(k).wait_send()
-        fwd_copy(k).wait_send()
         for p in range(len(downs)):
             second_copy(p, k).wait_send()
         return 0
@@ -327,16 +392,7 @@
     wide = 2 * dk
     nq = queries.shape[-1] // wide
     pairs = page_len // wide
-    device = lax.axis_index(("dp", "ep"))
-    own_lengths = lax.dynamic_slice_in_dim(lengths, device * slots, slots, 0)
-    own_move = lax.dynamic_slice_in_dim(move_slot, device, 1, 0)
-    scal = jnp.concatenate([own_move, own_lengths])
-    kv = jnp.pad(kv_new.reshape(slots, 1, dk), ((0, 0), (0, 15), (0, wide - dk)))
-    qk = jnp.concatenate([queries.reshape(slots, nq, wide), kv], axis=1)
-    hid = hidden.reshape(own_tok * CH, d_model // CH)
-    ids = expert_ids.reshape(n_dp, n_ep, own_tok, -1).transpose(1, 0, 2, 3).reshape(ntok, -1)
-    index = jnp.arange(pairs * pages, dtype=jnp.int32)
-    pos = jnp.broadcast_to((index % pages * (2 * pairs) + index // pages * 2)[None], (8, pairs * pages))
+    win = (dk + 127) // 128 * 128
     wmax = max(WIDTHS)
     np_ = len(WIDTHS)
     rchunk = min(rows, 256)
@@ -348,9 +404,9 @@
         functools.partial(kernel, n_dp, rchunk),
         out_shape=(
             jax.ShapeDtypeStruct((slots, nq, 2 * DL), BF16),
-            jax.ShapeDtypeStruct((own_tok, d_model), F32),
+            jax.ShapeDtypeStruct((own_tok, d_model), BF16),
         ),
-        in_specs=[pl.BlockSpec(memory_space=pltpu.SMEM), vm, vm, vm, vm] + [hb] * 8,
+        in_specs=[pl.BlockSpec(memory_space=pltpu.SMEM)] * 2 + [vm] * 4 + [hb] * 8,
         out_specs=(vm, vm),
         scratch_shapes=[
             pltpu.VMEM(cache.shape, BF16),
@@ -358,13 +414,17 @@
             pltpu.VMEM((all_rows, d_model), BF16),
             pltpu.VMEM((all_rows, d_model), BF16),
             pltpu.VMEM((all_rows, d_model), BF16),
+            pltpu.VMEM((d_model // CH // 128, own_tok * CH, 128), F32),
+            pltpu.VMEM((own_tok * CH, d_model // CH), BF16),
             pltpu.VMEM((n_ep, n_dp, own_tok * CH, d_model // CH), BF16),
             pltpu.VMEM((d_model // CH // 128, ntok * CH, 128), F32),
             pltpu.VMEM((ntok, d_model), BF16),
             pltpu.VMEM((ntok, all_rows), BF16),
             pltpu.VMEM((pairs * pages, wide), BF16),
-            pltpu.VMEM((nq + 16, wide), BF16),
-            pltpu.VMEM((nq + 16, wide), BF16),
+            pltpu.VMEM((nq, wide), BF16),
+            pltpu.VMEM((nq, wide), BF16),
+            pltpu.VMEM((16, win), BF16),
+            pltpu.VMEM((16, win), BF16),
             pltpu.VMEM((nq, 2 * DL), BF16),
             pltpu.VMEM((nq, 2 * DL), BF16),
             pltpu.VMEM((ntok, d_model), BF16),
@@ -375,15 +435,16 @@
         ]
         + [pltpu.VMEM((n_dp, own_tok * CH, w), BF16) for w in WIDTHS] * 2
         + [
-            dma((ncopy,)), dma((n_dp,)), dma((n_dp,)), dma((n_ep, n_dp)),
-            dma, dma, dma, dma,
+            dma((ncopy,)), dma((n_dp,)), dma((n_dp,)), dma((n_dp,)), dma((n_ep, n_dp)),
+            dma, dma, dma, dma, dma, dma,
             dma((np_,)), dma((np_,)), dma((np_, n_dp)), dma((np_, n_dp)),
         ],
         compiler_params=pltpu.CompilerParams(
             collective_id=0, has_side_effects=True, vmem_limit_bytes=63 * 1024 * 1024),
-    )(scal, qk, hid, ids, pos, cache, router, routed_gate, routed_up, routed_down,
+    )(lengths, move_slot, queries.reshape(slots, nq, wide), kv_new.reshape(slots, dk),
+      hidden.reshape(own_tok, d_model), expert_ids.reshape(ntok, -1).T, cache, router, routed_gate, routed_up, routed_down,
       shared_gate, shared_up, shared_down)
-    return (attn.reshape(slots, 1, nq * 2 * DL), moe.astype(BF16).reshape(hidden.shape))
+    return (attn.reshape(slots, 1, nq * 2 * DL), moe.reshape(hidden.shape))
 
 
 def solution(mesh):

time: 63.9 us -> 53.1 us (0.83)
  local copies, waits for them, and re-layouts: 8.86 us -> 4.93 us
  other arithmetic: 3.46 us -> 0 us
  Pallas kernels: 50.5 us -> 47.3 us
    pallas_call x1, Pallas kernels: 50.5 us -> 47.3 us  [local(): pl.pallas_call(functools.partial(kernel, n_dp, rchunk), out_shape=(jax.Sh...]
    concatenate x2 -> x0, other arithmetic: 2 us -> none  [the longest x1 1.24 us: local(): scal = jnp.concatenate([own_move, own_lengths])]
    dynamic_slice x2 -> x0, local copies, waits for them, and re-layouts: 1.97 us -> none  [the longest x1 1.24 us: local(): own_move = lax.dynamic_slice_in_dim(move_slot, device, 1, 0)]
    reshape x1 -> x0, other arithmetic: 1.45 us -> none  [local(): moe.astype(BF16).reshape(hidden.shape)]
    reshape x2 -> x1, local copies, waits for them, and re-layouts: 3.23 us -> 1.85 us  [local(): return (attn.reshape(slots, 1, nq * 2 * DL), moe.reshape(hidden.shape))]
    unnamed x3 -> x2, local copies, waits for them, and re-layouts: 2.44 us -> 3.08 us
where the time goes in v1:
time: 53.1 us; the launch traced here: 52.8 us
  Pallas kernels  47.3 us (89%)
  local copies, waits for them, and re-layouts  4.93 us (9%)
  between operations  0.64 us (1%)
    pallas_call x1, Pallas kernels, local(): pl.pallas_call(functools.partial(kernel, n_dp, rchunk), out_shape=(jax.Sh...  47.3 us
    unnamed x2, local copies, waits for them, and re-layouts  3.08 us
    reshape x1, local copies, waits for them, and re-layouts, local(): return (attn.reshape(slots, 1, nq * 2 * DL), moe.reshape(hidden.shape))  1.85 us

profile of v1, /device:TPU:0, one launch (start us, length us, event | category | flops | bytes accessed | tf_op | source)
XLA Modules:
  0.0 52.8 jit_solution(3156803865796451587)
XLA Ops:
  0.6 1.7 %copy.18 = bf16[1,2,64,1152]{3,2,1,0:T(8,128)(2,1)} copy(bf16[1,2,64,1152]{3,1,2,0:T(2,128)(2,1)} %bitcast.13) | data formatting | bytes 589824
  2.3 47.3 %shard_map.149 = (bf16[2,64,1024]{2,1,0:T(8,128)(2,1)}, bf16[2,7168]{1,0:T(2,128)(2,1)}) custom-call(s32[32]{0:T(128)} %len_ref.1, s32[16]{0:T(128)} %move_ref.1, bf16[2,64,1152]{2,1,0:T(8,128)(2,1)} %bitcast.12, bf16[2,576]{1,0:T(2,128)(2,1)} %bitcast.17, bf16[2,7168]{1,0:T(2,128)(2,1)} %bitcast.14, s32[8,32]{1,0:T(8,128)} %bitcast.16, ...), custom_call_target="tpu_custom_call" | custom-call | tf_op jit(solution)/shard_map/pallas_call | solution.py:403
  49.6 1.9 %reshape.26 = bf16[2,1,65536]{2,0,1:T(2,128)(2,1)} reshape(bf16[2,64,1024]{2,1,0:T(8,128)(2,1)} %get-tuple-element.4) | data formatting | bytes 524288 | tf_op jit(solution)/shard_map/reshape | solution.py:447
  51.4 1.4 %copy.20 = bf16[2,1,7168]{2,0,1:T(2,128)(2,1)} copy(bf16[2,1,7168]{2,0,1:T(2,128)(2,1)} %bitcast.15) | data formatting | bytes 57344

commit v2 on v1

--- a/solution.py
+++ b/solution.py
@@ -13,7 +13,7 @@
 ROUTE_SCALE = 2.5
 NEGATIVE = -1e30
 CH = 8
-WIDTHS = (384, 256, 256)
+WIDTHS = (384, 384, 128)
 MESH = pl.DeviceIdType.MESH
 F32 = jnp.float32
 BF16 = jnp.bfloat16

time: 53.1 us -> 53.7 us (1.011)
  Pallas kernels: 47.3 us -> 47.9 us
    pallas_call x1, Pallas kernels: 47.3 us -> 47.9 us  [local(): pl.pallas_call(functools.partial(kernel, n_dp, rchunk), out_shape=(jax.Sh...]
where the time goes in v2:
time: 53.7 us; the launch traced here: 53.5 us
  Pallas kernels  47.9 us (89%)
  local copies, waits for them, and re-layouts  4.93 us (9%)
  between operations  0.64 us (1%)
    pallas_call x1, Pallas kernels, local(): pl.pallas_call(functools.partial(kernel, n_dp, rchunk), out_shape=(jax.Sh...  47.9 us
    unnamed x2, local copies, waits for them, and re-layouts  3.08 us
    reshape x1, local copies, waits for them, and re-layouts, local(): return (attn.reshape(slots, 1, nq * 2 * DL), moe.reshape(hidden.shape))  1.85 us

profile of v2, /device:TPU:0, one launch (start us, length us, event | category | flops | bytes accessed | tf_op | source)
XLA Modules:
  0.0 53.5 jit_solution(9739757838804598015)
XLA Ops:
  0.6 1.7 %copy.18 = bf16[1,2,64,1152]{3,2,1,0:T(8,128)(2,1)} copy(bf16[1,2,64,1152]{3,1,2,0:T(2,128)(2,1)} %bitcast.13) | data formatting | bytes 589824
  2.3 47.9 %shard_map.149 = (bf16[2,64,1024]{2,1,0:T(8,128)(2,1)}, bf16[2,7168]{1,0:T(2,128)(2,1)}) custom-call(s32[32]{0:T(128)} %len_ref.1, s32[16]{0:T(128)} %move_ref.1, bf16[2,64,1152]{2,1,0:T(8,128)(2,1)} %bitcast.12, bf16[2,576]{1,0:T(2,128)(2,1)} %bitcast.17, bf16[2,7168]{1,0:T(2,128)(2,1)} %bitcast.14, s32[8,32]{1,0:T(8,128)} %bitcast.16, ...), custom_call_target="tpu_custom_call" | custom-call | tf_op jit(solution)/shard_map/pallas_call | solution.py:403
  50.3 1.9 %reshape.26 = bf16[2,1,65536]{2,0,1:T(2,128)(2,1)} reshape(bf16[2,64,1024]{2,1,0:T(8,128)(2,1)} %get-tuple-element.4) | data formatting | bytes 524288 | tf_op jit(solution)/shard_map/reshape | solution.py:447
  52.1 1.4 %copy.20 = bf16[2,1,7168]{2,0,1:T(2,128)(2,1)} copy(bf16[2,1,7168]{2,0,1:T(2,128)(2,1)} %bitcast.15) | data formatting | bytes 57344
